TPU v7x, 128 devices: a whole 4x4x4 slice. The times are simulated.
128 devices in a mesh: dp: 16 (over z, y_hi, core), mp: 8 (over y_lo, x).
Axes of the slice: x: 4, y: 4 (y_hi: 2, y_lo: 2; y = y_hi * 2 + y_lo), z: 4, core: 2. Of those that a mesh axis runs over, the one named last changes fastest.
Arguments:
- picture_summary_vectors: bfloat16 [16384, 1152], P(('dp', 'mp')), may hold values from -6 to 6
- caption_summary_vectors: bfloat16 [16384, 1152], P(('dp', 'mp')), may hold values from -6 to 6
- picture_mapping_matrix: bfloat16 [1152, 1152], P(('dp', 'mp')), may hold values from -0.1875 to 0.1875
- caption_mapping_matrix: bfloat16 [1152, 1152], P(('dp', 'mp')), may hold values from -0.1875 to 0.1875
- picture_partner_label: int32 [16384], P(('dp', 'mp')), may hold values from 0 to 4095
- caption_partner_label: int32 [16384], P(('dp', 'mp')), may hold values from 0 to 4095
- similarity_factor: float32 [1], replicated, may hold values from 5 to 15
- offset_term: float32 [1], replicated, may hold values from -4 to -1
Outputs:
- img_grad: bfloat16 [16384, 1152], P(('dp', 'mp'))
- txt_grad: bfloat16 [16384, 1152], P(('dp', 'mp'))
- w_img_grad: float32 [1152, 1152], P(('dp', 'mp'))
- w_txt_grad: float32 [1152, 1152], P(('dp', 'mp'))
All inputs are finite; a program needn't handle non-finite values.
Results may differ from a plain program's by a relative error of at most 0.023.
Values may be sent and summed in bfloat16 or wider, within the bound.
No kernel may reach another device: no remote copies, remote signals or barrier semaphores. Data moves between devices by JAX's collectives and lax.ppermute only.
A program may use at most 128 MiB of HBM per device.

v0:
```python
import jax
import jax.numpy as jnp
from jax import lax
from jax.sharding import PartitionSpec as P


def passed_along(value, axis, steps):
    count = lax.axis_size(axis)
    pairs = [(source, (source + steps) % count) for source in range(count)]
    return lax.ppermute(value, axis, pairs)


def embed(feat, weight):
    pre = jnp.dot(feat, weight, preferred_element_type=jnp.float32)
    radius = jnp.sqrt(jnp.sum(pre * pre, axis=1, keepdims=True) + 1e-06)
    return (pre / radius, radius)


def pair_terms(big_emb, big_ids, text_emb, text_ids, similarity_multiplier, offset):
    logits = (
        similarity_multiplier
        * lax.dot_general(
            big_emb, text_emb, (((1,), (1,)), ((), ())), preferred_element_type=jnp.float32
        )
        + offset
    )
    sign = jnp.where(big_ids[:, None] == text_ids[None, :], 1.0, -1.0).astype(jnp.float32)
    slope = (-sign * jax.nn.sigmoid(-sign * logits)).astype(jnp.bfloat16)
    image_part = jnp.dot(slope, text_emb, preferred_element_type=jnp.float32)
    text_part = lax.dot_general(
        slope, big_emb, (((0,), (0,)), ((), ())), preferred_element_type=jnp.float32
    )
    return (image_part, text_part)


def backward_rows(unit, radius, grad, feat, weight):
    d_pre = ((grad - unit * jnp.sum(unit * grad, axis=1, keepdims=True)) / radius).astype(
        jnp.bfloat16
    )
    d_feat = lax.dot_general(
        d_pre, weight, (((1,), (1,)), ((), ())), preferred_element_type=jnp.float32
    ).astype(jnp.bfloat16)
    d_weight = lax.dot_general(
        feat, d_pre, (((0,), (0,)), ((), ())), preferred_element_type=jnp.float32
    )
    return (d_feat, d_weight)


def on_device(
    picture_summary_vectors,
    caption_summary_vectors,
    picture_mapping_matrix,
    caption_mapping_matrix,
    picture_partner_label,
    caption_partner_label,
    similarity_factor,
    offset_term,
):
    full_img, full_txt = (
        lax.all_gather(picture_mapping_matrix, ("dp", "mp"), axis=0, tiled=True),
        lax.all_gather(caption_mapping_matrix, ("dp", "mp"), axis=0, tiled=True),
    )
    unit_img, rad_img = embed(picture_summary_vectors, full_img)
    unit_txt, rad_txt = embed(caption_summary_vectors, full_txt)
    emb_img = unit_img.astype(jnp.bfloat16)
    emb_txt = unit_txt.astype(jnp.bfloat16)
    big_emb, big_ids = (
        lax.all_gather(emb_img, "mp", axis=0, tiled=True),
        lax.all_gather(picture_partner_label, "mp", axis=0, tiled=True),
    )
    similarity_multiplier = similarity_factor[0]
    offset = offset_term[0]
    rows = emb_txt.shape[0]
    width = emb_txt.shape[1]
    turns = lax.axis_size("dp")
    image_sum = jnp.zeros((big_emb.shape[0], width), jnp.float32)

    def turn(step, carry):
        image_total, text_emb, text_ids, text_total = carry
        image_part, text_part = pair_terms(
            big_emb, big_ids, text_emb, text_ids, similarity_multiplier, offset
        )
        image_total = image_total + image_part
        text_total = text_total + text_part
        text_emb, text_ids = passed_along((text_emb, text_ids), "dp", 1)
        text_total = passed_along(text_total, "dp", 1)
        return (image_total, text_emb, text_ids, text_total)

    start = (image_sum, emb_txt, caption_partner_label, jnp.zeros((rows, width), jnp.float32))
    image_sum, moved_emb, moved_ids, text_sum = lax.fori_loop(0, turns, turn, start)
    d_emb_txt = similarity_multiplier * text_sum
    d_emb_img = similarity_multiplier * lax.psum_scatter(
        image_sum.astype(jnp.bfloat16), "mp", scatter_dimension=0, tiled=True
    ).astype(jnp.float32)
    img_grad, d_w_img = backward_rows(
        unit_img, rad_img, d_emb_img, picture_summary_vectors, full_img
    )
    txt_grad, d_w_txt = backward_rows(
        unit_txt, rad_txt, d_emb_txt, caption_summary_vectors, full_txt
    )
    w_img_grad, w_txt_grad = (
        lax.psum_scatter(d_w_img, ("dp", "mp"), scatter_dimension=0, tiled=True),
        lax.psum_scatter(d_w_txt, ("dp", "mp"), scatter_dimension=0, tiled=True),
    )
    return (img_grad, txt_grad, w_img_grad, w_txt_grad)


def solution(mesh):
    in_specs = (
        P(("dp", "mp"), None),
        P(("dp", "mp"), None),
        P(("dp", "mp"), None),
        P(("dp", "mp"), None),
        P(("dp", "mp")),
        P(("dp", "mp")),
        P(),
        P(),
    )
    out_specs = (
        P(("dp", "mp"), None),
        P(("dp", "mp"), None),
        P(("dp", "mp"), None),
        P(("dp", "mp"), None),
    )
    return jax.shard_map(
        on_device, mesh=mesh, in_specs=in_specs, out_specs=out_specs, check_vma=False
    )
```

profile of v0, /device:TPU:1, one launch (start us, length us, event | category | flops | bytes accessed | tf_op | source)
XLA Modules:
  0.0 1233.9 jit_solution(1294834546213781701)
XLA Ops:
  8.7 312.7 %all-gather.11.cloned.1.call-done = bf16[128,9,1152]{2,1,0:T(8,128)(2,1)} async-done(((bf16[1,9,1152]{2,1,0:T(8,128)(2,1)}), bf16[128,9,1152]{2,1,0:T(8,128)(2,1)}) %all-gather.11.cloned.1.call-update) | async-done | bytes 2654224 | tf_op jit(solution)/shard_map/all_gather | solution.py:60
  321.4 4.3 reshape.29
  328.4 14.2 %all-gather.1 = s32[8,1,128]{2,1,0:T(1,128)S(1)} all-gather(s32[1,1,128]{2,1,0:T(1,128)S(1)} %bitcast.49), channel_id=1, replica_groups=mesh['dp'=16,'mp'=8] {'mp'}, dimensions={0}, use_global_device_ids=true | all-gather | bytes 4608 | tf_op jit(solution)/shard_map/all_gather | solution.py:69
  342.7 290.6 %all-gather.9.cloned.1.call-done = bf16[128,9,1152]{2,1,0:T(8,128)(2,1)} async-done(((bf16[1,9,1152]{2,1,0:T(8,128)(2,1)}), bf16[128,9,1152]{2,1,0:T(8,128)(2,1)}) %all-gather.9.cloned.1.call-update) | async-done | bytes 2654224 | tf_op jit(solution)/shard_map/all_gather | solution.py:61
  633.2 5.8 reshape.25
  641.6 31.5 %all-gather.7.cloned.1.call-done = bf16[1024,1152]{1,0:T(8,128)(2,1)} async-done(((bf16[128,1152]{1,0:T(8,128)(2,1)}), bf16[1024,1152]{1,0:T(8,128)(2,1)}) %all-gather.7.cloned.1.call-update) | async-done | bytes 2359312 | tf_op jit(solution)/shard_map/all_gather | solution.py:68
  673.2 324.3 %while.17 = (s32[]{:T(128)}, f32[1024,1152]{1,0:T(8,128)}, bf16[128,1152]{1,0:T(8,128)(2,1)S(1)}, s32[128]{0:T(128)S(1)}, f32[128,1152]{1,0:T(8,128)S(1)}, /*ind...) while((s32[]{:T(128)}, f32[1024,1152]{1,0:T(8,128)}, ...), condition=%wide.region_3.4_spmd.clone, body=%wide.region_2.3_spmd.clone.sunk | while | flops 909918208 | bytes 30285588 | solution.py:90
  673.3 4.0 fusion.37
  677.8 7.4 collective-permute-start.2
  690.1 5.2 collective-permute-done.1
  695.3 4.0 fusion.37
  699.8 4.1 collective-permute-start.2
  706.7 5.3 convolution_add_fusion.4
  714.0 4.0 fusion.37
  718.6 4.1 collective-permute-start.2
  726.4 5.3 convolution_add_fusion.4
  732.7 4.0 fusion.37
  737.3 4.1 collective-permute-start.2
  741.4 4.5 collective-permute-start.1
  746.0 5.3 convolution_add_fusion.4
  751.4 4.0 fusion.37
  756.0 4.1 collective-permute-start.2
  760.7 4.9 collective-permute-start.1
  765.6 5.3 convolution_add_fusion.4
  770.9 4.0 fusion.37
  780.3 4.9 collective-permute-start.1
  785.2 5.3 convolution_add_fusion.4
  790.6 4.0 fusion.37
  799.9 4.9 collective-permute-start.1
  804.8 5.3 convolution_add_fusion.4
  810.2 4.0 fusion.37
  819.5 4.9 collective-permute-start.1
  824.4 5.3 convolution_add_fusion.4
  831.0 4.0 fusion.37
  839.1 4.9 collective-permute-start.1
  844.0 5.3 convolution_add_fusion.4
  851.8 4.0 fusion.37
  858.7 4.9 collective-permute-start.1
  863.6 5.3 convolution_add_fusion.4
  868.9 3.7 collective-permute-done.1
  872.6 4.0 fusion.37
  878.4 4.9 collective-permute-start.1
  883.3 5.3 convolution_add_fusion.4
  888.5 4.9 collective-permute-done.1
  893.5 4.0 fusion.37
  898.2 4.7 collective-permute-start.1
  902.9 5.3 convolution_add_fusion.4
  908.2 6.1 collective-permute-done.1
  914.3 4.0 fusion.37
  922.5 5.3 convolution_add_fusion.4
  927.8 7.3 collective-permute-done.1
  935.1 4.0 fusion.37
  942.1 5.3 convolution_add_fusion.4
  947.4 8.5 collective-permute-done.1
  955.9 4.0 fusion.37
  961.7 5.3 convolution_add_fusion.4
  967.0 9.7 collective-permute-done.1
  976.7 4.0 fusion.37
  981.6 5.3 convolution_add_fusion.4
  986.9 10.7 collective-permute-done.1
  997.5 4.0 convert_element_type.29
  1005.8 42.9 %reduce-scatter.4.cloned.1.call-done = bf16[128,1152]{1,0:T(8,128)(2,1)} async-done(((bf16[1024,1152]{1,0:T(8,128)(2,1)}), bf16[128,1152]{1,0:T(8,128)(2,1)}) %reduce-scatter.4.cloned.1.call-update) | async-done | bytes 294928 | tf_op jit(solution)/shard_map/reduce_scatter | solution.py:92
  1049.9 4.2 convolution_bitcast_fusion.1
  1060.5 163.2 %all-reduce.5.cloned.1.call-done = (f32[1152,1152]{0,1:T(8,128)}, f32[1152,1152]{0,1:T(8,128)}) async-done(((f32[1152,1152]{0,1:T(8,128)}, f32[1152,1152]{0,1:T(8,128)}), (f32[1152,1152]{0,1:T(8,128)}, f32[1152,1152]{0,1:T(8,128)})) %all-reduce.5.cloned.1.call-update) | async-done | bytes 10616848
  (207 shorter events, 78.7 us)
Async XLA Ops:
  7.2 631.9 %copy-start = (bf16[128,1152]{1,0:T(8,128)(2,1)S(1)}, bf16[128,1152]{1,0:T(8,128)(2,1)}, u32[]{:S(2)}) copy-start(bf16[128,1152]{1,0:T(8,128)(2,1)} %param.11) | copy-start | bytes 884740
  7.2 314.3 %all-gather.11.cloned.1.call-start = ((), (), s32[]{:S(2)}) async-start(), calls=%async_computation.4 | async-start | bytes 4755456 | tf_op jit(solution)/shard_map/all_gather | solution.py:60
  7.9 625.3 %all-gather.9.cloned.1.call-start = ((), (), s32[]{:S(2)}) async-start(), calls=%async_computation.3 | async-start | bytes 4755456 | tf_op jit(solution)/shard_map/all_gather | solution.py:61
  8.7 317.1 %copy-start.9 = (bf16[128,1152]{1,0:T(8,128)(2,1)S(1)}, bf16[128,1152]{1,0:T(8,128)(2,1)}, u32[]{:S(2)}) copy-start(bf16[128,1152]{1,0:T(8,128)(2,1)} %param.10) | copy-start | bytes 884740
  8.7 664.5 %all-gather.7.cloned.1.call-start = ((), (), s32[]{:S(2)}) async-start(), calls=%async_computation.1 | async-start | bytes 2654208 | tf_op jit(solution)/shard_map/all_gather | solution.py:68
  325.8 313.2 %copy-start.2 = (bf16[1152,1152]{1,0:T(8,128)(2,1)}, bf16[1152,1152]{1,0:T(8,128)(2,1)S(1)}, u32[]{:S(2)}) copy-start(bf16[1152,1152]{1,0:T(8,128)(2,1)S(1)} %reshape.29) | copy-start | bytes 7962628
  328.4 720.4 %reduce-scatter.4.cloned.1.call-start = ((), (), s32[]{:S(2)}) async-start(), calls=%async_computation.2 | async-start | bytes 2654208 | tf_op jit(solution)/shard_map/reduce_scatter | solution.py:92
  639.0 34.2 %copy-start.13 = (s32[128]{0:T(128)S(1)}, s32[128]{0:T(128)}, u32[]{:S(2)}) copy-start(s32[128]{0:T(128)} %param.15) | copy-start | bytes 1540
  641.5 361.0 %copy-start.5 = (f32[128,1152]{1,0:T(8,128)}, f32[128,1152]{1,0:T(8,128)S(1)}, u32[]{:S(2)}) copy-start(f32[128,1152]{1,0:T(8,128)S(1)} %get-tuple-element.117) | copy-start | bytes 1769476
  677.8 17.4 %collective-permute-start.2 = (f32[128,1152]{1,0:T(8,128)S(1)}, f32[128,1152]{1,0:T(8,128)S(1)}, u32[]{:S(2)}, u32[]{:S(2)}) collective-permute-start(f32[128,1152]{1,0:T(8,128)S(1)} %convolution_add_fusion.5), channel_id=1, source_target_pairs={{0,8},{8,16},{16,24},{24,32},{32,40},{40,48},{48,56},{56,64},{64,7... | collective-permute-start | bytes 1769480 | tf_op jit(solution)/shard_map/while/body/eval_jaxpr/ppermute | solution.py:10
  685.2 10.0 collective-permute-start
  685.3 9.9 collective-permute-start.1
  699.8 14.1 %collective-permute-start.2 = (f32[128,1152]{1,0:T(8,128)S(1)}, f32[128,1152]{1,0:T(8,128)S(1)}, u32[]{:S(2)}, u32[]{:S(2)}) collective-permute-start(f32[128,1152]{1,0:T(8,128)S(1)} %convolution_add_fusion.5), channel_id=1, source_target_pairs={{0,8},{8,16},{16,24},{24,32},{32,40},{40,48},{48,56},{56,64},{64,7... | collective-permute-start | bytes 1769480 | tf_op jit(solution)/shard_map/while/body/eval_jaxpr/ppermute | solution.py:10
  703.9 10.0 collective-permute-start
  704.0 9.9 collective-permute-start.1
  714.0 4.0 copy-start.1
  718.6 14.1 %collective-permute-start.2 = (f32[128,1152]{1,0:T(8,128)S(1)}, f32[128,1152]{1,0:T(8,128)S(1)}, u32[]{:S(2)}, u32[]{:S(2)}) collective-permute-start(f32[128,1152]{1,0:T(8,128)S(1)} %convolution_add_fusion.5), channel_id=1, source_target_pairs={{0,8},{8,16},{16,24},{24,32},{32,40},{40,48},{48,56},{56,64},{64,7... | collective-permute-start | bytes 1769480 | tf_op jit(solution)/shard_map/while/body/eval_jaxpr/ppermute | solution.py:10
  722.6 10.0 collective-permute-start
  722.7 9.9 collective-permute-start.1
  737.3 14.1 %collective-permute-start.2 = (f32[128,1152]{1,0:T(8,128)S(1)}, f32[128,1152]{1,0:T(8,128)S(1)}, u32[]{:S(2)}, u32[]{:S(2)}) collective-permute-start(f32[128,1152]{1,0:T(8,128)S(1)} %convolution_add_fusion.5), channel_id=1, source_target_pairs={{0,8},{8,16},{16,24},{24,32},{32,40},{40,48},{48,56},{56,64},{64,7... | collective-permute-start | bytes 1769480 | tf_op jit(solution)/shard_map/while/body/eval_jaxpr/ppermute | solution.py:10
  741.3 10.0 collective-permute-start
  741.4 9.9 collective-permute-start.1
  756.0 14.9 %collective-permute-start.2 = (f32[128,1152]{1,0:T(8,128)S(1)}, f32[128,1152]{1,0:T(8,128)S(1)}, u32[]{:S(2)}, u32[]{:S(2)}) collective-permute-start(f32[128,1152]{1,0:T(8,128)S(1)} %convolution_add_fusion.5), channel_id=1, source_target_pairs={{0,8},{8,16},{16,24},{24,32},{32,40},{40,48},{48,56},{56,64},{64,7... | collective-permute-start | bytes 1769480 | tf_op jit(solution)/shard_map/while/body/eval_jaxpr/ppermute | solution.py:10
  760.1 10.8 collective-permute-start
  760.7 10.2 collective-permute-start.1
  775.5 15.0 %collective-permute-start.2 = (f32[128,1152]{1,0:T(8,128)S(1)}, f32[128,1152]{1,0:T(8,128)S(1)}, u32[]{:S(2)}, u32[]{:S(2)}) collective-permute-start(f32[128,1152]{1,0:T(8,128)S(1)} %convolution_add_fusion.5), channel_id=1, source_target_pairs={{0,8},{8,16},{16,24},{24,32},{32,40},{40,48},{48,56},{56,64},{64,7... | collective-permute-start | bytes 1769480 | tf_op jit(solution)/shard_map/while/body/eval_jaxpr/ppermute | solution.py:10
  778.8 11.7 collective-permute-start
  780.3 10.2 collective-permute-start.1
  790.5 4.0 copy-start.1
  795.1 15.0 %collective-permute-start.2 = (f32[128,1152]{1,0:T(8,128)S(1)}, f32[128,1152]{1,0:T(8,128)S(1)}, u32[]{:S(2)}, u32[]{:S(2)}) collective-permute-start(f32[128,1152]{1,0:T(8,128)S(1)} %convolution_add_fusion.5), channel_id=1, source_target_pairs={{0,8},{8,16},{16,24},{24,32},{32,40},{40,48},{48,56},{56,64},{64,7... | collective-permute-start | bytes 1769480 | tf_op jit(solution)/shard_map/while/body/eval_jaxpr/ppermute | solution.py:10
  797.5 12.6 %collective-permute-start = (bf16[128,1152]{1,0:T(8,128)(2,1)S(1)}, bf16[128,1152]{1,0:T(8,128)(2,1)S(1)}, u32[]{:S(2)}, u32[]{:S(2)}) collective-permute-start(bf16[128,1152]{1,0:T(8,128)(2,1)S(1)} %copy.29), channel_id=1, source_target_pairs={{0,8},{8,16},{16,24},{24,32},{32,40},{40,48},{48,56},{56,64},{64,7... | collective-permute-start | bytes 884744 | tf_op jit(solution)/shard_map/while/body/eval_jaxpr/ppermute | solution.py:10
  799.9 10.2 collective-permute-start.1
  814.7 16.2 %collective-permute-start.2 = (f32[128,1152]{1,0:T(8,128)S(1)}, f32[128,1152]{1,0:T(8,128)S(1)}, u32[]{:S(2)}, u32[]{:S(2)}) collective-permute-start(f32[128,1152]{1,0:T(8,128)S(1)} %convolution_add_fusion.5), channel_id=1, source_target_pairs={{0,8},{8,16},{16,24},{24,32},{32,40},{40,48},{48,56},{56,64},{64,7... | collective-permute-start | bytes 1769480 | tf_op jit(solution)/shard_map/while/body/eval_jaxpr/ppermute | solution.py:10
  816.2 14.8 %collective-permute-start = (bf16[128,1152]{1,0:T(8,128)(2,1)S(1)}, bf16[128,1152]{1,0:T(8,128)(2,1)S(1)}, u32[]{:S(2)}, u32[]{:S(2)}) collective-permute-start(bf16[128,1152]{1,0:T(8,128)(2,1)S(1)} %copy.29), channel_id=1, source_target_pairs={{0,8},{8,16},{16,24},{24,32},{32,40},{40,48},{48,56},{56,64},{64,7... | collective-permute-start | bytes 884744 | tf_op jit(solution)/shard_map/while/body/eval_jaxpr/ppermute | solution.py:10
  819.5 11.4 collective-permute-start.1
  835.6 16.2 %collective-permute-start.2 = (f32[128,1152]{1,0:T(8,128)S(1)}, f32[128,1152]{1,0:T(8,128)S(1)}, u32[]{:S(2)}, u32[]{:S(2)}) collective-permute-start(f32[128,1152]{1,0:T(8,128)S(1)} %convolution_add_fusion.5), channel_id=1, source_target_pairs={{0,8},{8,16},{16,24},{24,32},{32,40},{40,48},{48,56},{56,64},{64,7... | collective-permute-start | bytes 1769480 | tf_op jit(solution)/shard_map/while/body/eval_jaxpr/ppermute | solution.py:10
  835.6 16.1 %collective-permute-start = (bf16[128,1152]{1,0:T(8,128)(2,1)S(1)}, bf16[128,1152]{1,0:T(8,128)(2,1)S(1)}, u32[]{:S(2)}, u32[]{:S(2)}) collective-permute-start(bf16[128,1152]{1,0:T(8,128)(2,1)S(1)} %copy.29), channel_id=1, source_target_pairs={{0,8},{8,16},{16,24},{24,32},{32,40},{40,48},{48,56},{56,64},{64,7... | collective-permute-start | bytes 884744 | tf_op jit(solution)/shard_map/while/body/eval_jaxpr/ppermute | solution.py:10
  839.1 12.6 %collective-permute-start.1 = (s32[128]{0:T(128)S(1)}, s32[128]{0:T(128)S(1)}, u32[]{:S(2)}, u32[]{:S(2)}) collective-permute-start(s32[128]{0:T(128)S(1)} %copy.30), channel_id=1, source_target_pairs={{0,8},{8,16},{16,24},{24,32},{32,40},{40,48},{48,56},{56,64},{64,7... | collective-permute-start | bytes 1544 | tf_op jit(solution)/shard_map/while/body/eval_jaxpr/ppermute | solution.py:10
  851.8 4.0 copy-start.1
  856.4 16.2 %collective-permute-start.2 = (f32[128,1152]{1,0:T(8,128)S(1)}, f32[128,1152]{1,0:T(8,128)S(1)}, u32[]{:S(2)}, u32[]{:S(2)}) collective-permute-start(f32[128,1152]{1,0:T(8,128)S(1)} %convolution_add_fusion.5), channel_id=1, source_target_pairs={{0,8},{8,16},{16,24},{24,32},{32,40},{40,48},{48,56},{56,64},{64,7... | collective-permute-start | bytes 1769480 | tf_op jit(solution)/shard_map/while/body/eval_jaxpr/ppermute | solution.py:10
  856.5 16.1 %collective-permute-start = (bf16[128,1152]{1,0:T(8,128)(2,1)S(1)}, bf16[128,1152]{1,0:T(8,128)(2,1)S(1)}, u32[]{:S(2)}, u32[]{:S(2)}) collective-permute-start(bf16[128,1152]{1,0:T(8,128)(2,1)S(1)} %copy.29), channel_id=1, source_target_pairs={{0,8},{8,16},{16,24},{24,32},{32,40},{40,48},{48,56},{56,64},{64,7... | collective-permute-start | bytes 884744 | tf_op jit(solution)/shard_map/while/body/eval_jaxpr/ppermute | solution.py:10
  858.7 13.9 %collective-permute-start.1 = (s32[128]{0:T(128)S(1)}, s32[128]{0:T(128)S(1)}, u32[]{:S(2)}, u32[]{:S(2)}) collective-permute-start(s32[128]{0:T(128)S(1)} %copy.30), channel_id=1, source_target_pairs={{0,8},{8,16},{16,24},{24,32},{32,40},{40,48},{48,56},{56,64},{64,7... | collective-permute-start | bytes 1544 | tf_op jit(solution)/shard_map/while/body/eval_jaxpr/ppermute | solution.py:10
  877.2 16.2 %collective-permute-start.2 = (f32[128,1152]{1,0:T(8,128)S(1)}, f32[128,1152]{1,0:T(8,128)S(1)}, u32[]{:S(2)}, u32[]{:S(2)}) collective-permute-start(f32[128,1152]{1,0:T(8,128)S(1)} %convolution_add_fusion.5), channel_id=1, source_target_pairs={{0,8},{8,16},{16,24},{24,32},{32,40},{40,48},{48,56},{56,64},{64,7... | collective-permute-start | bytes 1769480 | tf_op jit(solution)/shard_map/while/body/eval_jaxpr/ppermute | solution.py:10
  877.3 16.1 %collective-permute-start = (bf16[128,1152]{1,0:T(8,128)(2,1)S(1)}, bf16[128,1152]{1,0:T(8,128)(2,1)S(1)}, u32[]{:S(2)}, u32[]{:S(2)}) collective-permute-start(bf16[128,1152]{1,0:T(8,128)(2,1)S(1)} %copy.29), channel_id=1, source_target_pairs={{0,8},{8,16},{16,24},{24,32},{32,40},{40,48},{48,56},{56,64},{64,7... | collective-permute-start | bytes 884744 | tf_op jit(solution)/shard_map/while/body/eval_jaxpr/ppermute | solution.py:10
  878.4 15.1 %collective-permute-start.1 = (s32[128]{0:T(128)S(1)}, s32[128]{0:T(128)S(1)}, u32[]{:S(2)}, u32[]{:S(2)}) collective-permute-start(s32[128]{0:T(128)S(1)} %copy.30), channel_id=1, source_target_pairs={{0,8},{8,16},{16,24},{24,32},{32,40},{40,48},{48,56},{56,64},{64,7... | collective-permute-start | bytes 1544 | tf_op jit(solution)/shard_map/while/body/eval_jaxpr/ppermute | solution.py:10
  893.5 4.0 copy-start.1
  898.0 16.2 %collective-permute-start.2 = (f32[128,1152]{1,0:T(8,128)S(1)}, f32[128,1152]{1,0:T(8,128)S(1)}, u32[]{:S(2)}, u32[]{:S(2)}) collective-permute-start(f32[128,1152]{1,0:T(8,128)S(1)} %convolution_add_fusion.5), channel_id=1, source_target_pairs={{0,8},{8,16},{16,24},{24,32},{32,40},{40,48},{48,56},{56,64},{64,7... | collective-permute-start | bytes 1769480 | tf_op jit(solution)/shard_map/while/body/eval_jaxpr/ppermute | solution.py:10
  898.1 16.1 %collective-permute-start = (bf16[128,1152]{1,0:T(8,128)(2,1)S(1)}, bf16[128,1152]{1,0:T(8,128)(2,1)S(1)}, u32[]{:S(2)}, u32[]{:S(2)}) collective-permute-start(bf16[128,1152]{1,0:T(8,128)(2,1)S(1)} %copy.29), channel_id=1, source_target_pairs={{0,8},{8,16},{16,24},{24,32},{32,40},{40,48},{48,56},{56,64},{64,7... | collective-permute-start | bytes 884744 | tf_op jit(solution)/shard_map/while/body/eval_jaxpr/ppermute | solution.py:10
  898.2 16.0 %collective-permute-start.1 = (s32[128]{0:T(128)S(1)}, s32[128]{0:T(128)S(1)}, u32[]{:S(2)}, u32[]{:S(2)}) collective-permute-start(s32[128]{0:T(128)S(1)} %copy.30), channel_id=1, source_target_pairs={{0,8},{8,16},{16,24},{24,32},{32,40},{40,48},{48,56},{56,64},{64,7... | collective-permute-start | bytes 1544 | tf_op jit(solution)/shard_map/while/body/eval_jaxpr/ppermute | solution.py:10
  918.8 16.2 %collective-permute-start.2 = (f32[128,1152]{1,0:T(8,128)S(1)}, f32[128,1152]{1,0:T(8,128)S(1)}, u32[]{:S(2)}, u32[]{:S(2)}) collective-permute-start(f32[128,1152]{1,0:T(8,128)S(1)} %convolution_add_fusion.5), channel_id=1, source_target_pairs={{0,8},{8,16},{16,24},{24,32},{32,40},{40,48},{48,56},{56,64},{64,7... | collective-permute-start | bytes 1769480 | tf_op jit(solution)/shard_map/while/body/eval_jaxpr/ppermute | solution.py:10
  918.9 16.1 %collective-permute-start = (bf16[128,1152]{1,0:T(8,128)(2,1)S(1)}, bf16[128,1152]{1,0:T(8,128)(2,1)S(1)}, u32[]{:S(2)}, u32[]{:S(2)}) collective-permute-start(bf16[128,1152]{1,0:T(8,128)(2,1)S(1)} %copy.29), channel_id=1, source_target_pairs={{0,8},{8,16},{16,24},{24,32},{32,40},{40,48},{48,56},{56,64},{64,7... | collective-permute-start | bytes 884744 | tf_op jit(solution)/shard_map/while/body/eval_jaxpr/ppermute | solution.py:10
  919.0 16.1 %collective-permute-start.1 = (s32[128]{0:T(128)S(1)}, s32[128]{0:T(128)S(1)}, u32[]{:S(2)}, u32[]{:S(2)}) collective-permute-start(s32[128]{0:T(128)S(1)} %copy.30), channel_id=1, source_target_pairs={{0,8},{8,16},{16,24},{24,32},{32,40},{40,48},{48,56},{56,64},{64,7... | collective-permute-start | bytes 1544 | tf_op jit(solution)/shard_map/while/body/eval_jaxpr/ppermute | solution.py:10
  939.7 16.2 %collective-permute-start.2 = (f32[128,1152]{1,0:T(8,128)S(1)}, f32[128,1152]{1,0:T(8,128)S(1)}, u32[]{:S(2)}, u32[]{:S(2)}) collective-permute-start(f32[128,1152]{1,0:T(8,128)S(1)} %convolution_add_fusion.5), channel_id=1, source_target_pairs={{0,8},{8,16},{16,24},{24,32},{32,40},{40,48},{48,56},{56,64},{64,7... | collective-permute-start | bytes 1769480 | tf_op jit(solution)/shard_map/while/body/eval_jaxpr/ppermute | solution.py:10
  939.7 16.1 %collective-permute-start = (bf16[128,1152]{1,0:T(8,128)(2,1)S(1)}, bf16[128,1152]{1,0:T(8,128)(2,1)S(1)}, u32[]{:S(2)}, u32[]{:S(2)}) collective-permute-start(bf16[128,1152]{1,0:T(8,128)(2,1)S(1)} %copy.29), channel_id=1, source_target_pairs={{0,8},{8,16},{16,24},{24,32},{32,40},{40,48},{48,56},{56,64},{64,7... | collective-permute-start | bytes 884744 | tf_op jit(solution)/shard_map/while/body/eval_jaxpr/ppermute | solution.py:10
  939.8 16.0 %collective-permute-start.1 = (s32[128]{0:T(128)S(1)}, s32[128]{0:T(128)S(1)}, u32[]{:S(2)}, u32[]{:S(2)}) collective-permute-start(s32[128]{0:T(128)S(1)} %copy.30), channel_id=1, source_target_pairs={{0,8},{8,16},{16,24},{24,32},{32,40},{40,48},{48,56},{56,64},{64,7... | collective-permute-start | bytes 1544 | tf_op jit(solution)/shard_map/while/body/eval_jaxpr/ppermute | solution.py:10
  960.5 16.2 %collective-permute-start.2 = (f32[128,1152]{1,0:T(8,128)S(1)}, f32[128,1152]{1,0:T(8,128)S(1)}, u32[]{:S(2)}, u32[]{:S(2)}) collective-permute-start(f32[128,1152]{1,0:T(8,128)S(1)} %convolution_add_fusion.5), channel_id=1, source_target_pairs={{0,8},{8,16},{16,24},{24,32},{32,40},{40,48},{48,56},{56,64},{64,7... | collective-permute-start | bytes 1769480 | tf_op jit(solution)/shard_map/while/body/eval_jaxpr/ppermute | solution.py:10
  960.6 16.1 %collective-permute-start = (bf16[128,1152]{1,0:T(8,128)(2,1)S(1)}, bf16[128,1152]{1,0:T(8,128)(2,1)S(1)}, u32[]{:S(2)}, u32[]{:S(2)}) collective-permute-start(bf16[128,1152]{1,0:T(8,128)(2,1)S(1)} %copy.29), channel_id=1, source_target_pairs={{0,8},{8,16},{16,24},{24,32},{32,40},{40,48},{48,56},{56,64},{64,7... | collective-permute-start | bytes 884744 | tf_op jit(solution)/shard_map/while/body/eval_jaxpr/ppermute | solution.py:10
  960.6 16.1 %collective-permute-start.1 = (s32[128]{0:T(128)S(1)}, s32[128]{0:T(128)S(1)}, u32[]{:S(2)}, u32[]{:S(2)}) collective-permute-start(s32[128]{0:T(128)S(1)} %copy.30), channel_id=1, source_target_pairs={{0,8},{8,16},{16,24},{24,32},{32,40},{40,48},{48,56},{56,64},{64,7... | collective-permute-start | bytes 1544 | tf_op jit(solution)/shard_map/while/body/eval_jaxpr/ppermute | solution.py:10
  981.3 16.2 %collective-permute-start.2 = (f32[128,1152]{1,0:T(8,128)S(1)}, f32[128,1152]{1,0:T(8,128)S(1)}, u32[]{:S(2)}, u32[]{:S(2)}) collective-permute-start(f32[128,1152]{1,0:T(8,128)S(1)} %convolution_add_fusion.5), channel_id=1, source_target_pairs={{0,8},{8,16},{16,24},{24,32},{32,40},{40,48},{48,56},{56,64},{64,7... | collective-permute-start | bytes 1769480 | tf_op jit(solution)/shard_map/while/body/eval_jaxpr/ppermute | solution.py:10
  981.4 16.1 %collective-permute-start = (bf16[128,1152]{1,0:T(8,128)(2,1)S(1)}, bf16[128,1152]{1,0:T(8,128)(2,1)S(1)}, u32[]{:S(2)}, u32[]{:S(2)}) collective-permute-start(bf16[128,1152]{1,0:T(8,128)(2,1)S(1)} %copy.29), channel_id=1, source_target_pairs={{0,8},{8,16},{16,24},{24,32},{32,40},{40,48},{48,56},{56,64},{64,7... | collective-permute-start | bytes 884744 | tf_op jit(solution)/shard_map/while/body/eval_jaxpr/ppermute | solution.py:10
  981.5 16.0 %collective-permute-start.1 = (s32[128]{0:T(128)S(1)}, s32[128]{0:T(128)S(1)}, u32[]{:S(2)}, u32[]{:S(2)}) collective-permute-start(s32[128]{0:T(128)S(1)} %copy.30), channel_id=1, source_target_pairs={{0,8},{8,16},{16,24},{24,32},{32,40},{40,48},{48,56},{56,64},{64,7... | collective-permute-start | bytes 1544 | tf_op jit(solution)/shard_map/while/body/eval_jaxpr/ppermute | solution.py:10
  1001.5 222.2 %all-reduce.5.cloned.1.call-start = ((), (), s32[]{:S(2)}) async-start(), calls=%async_computation.5 | async-start | bytes 21233664
  1002.4 46.3 %copy-start.7 = (f32[128,1152]{1,0:T(8,128)S(1)}, f32[128,1152]{1,0:T(8,128)}, u32[]{:S(2)}) copy-start(f32[128,1152]{1,0:T(8,128)} %copy-done.6) | copy-start | bytes 1769476
  1002.5 47.5 %copy-start.10 = (bf16[128,1152]{1,0:T(8,128)(2,1)S(1)}, bf16[128,1152]{1,0:T(8,128)(2,1)}, u32[]{:S(2)}) copy-start(bf16[128,1152]{1,0:T(8,128)(2,1)} %param.10) | copy-start | bytes 884740
  (18 other events, 62.1 us)
Sparse Core Ops, SparseCore 0:
  9.7 311.6 all-gather.10
  323.1 310.0 all-gather.8
  635.4 37.6 all-gather.6
  1001.6 47.0 reduce-scatter.3
  1054.3 169.3 all-reduce.4
where the time goes:
time: 1240 us; the launch traced here: 1230 us
  waiting for transfers between devices  905 us (73%)
  matrix products  170 us (14%)
  starting transfers between devices  106 us (9%)
  local copies, waits for them, and re-layouts  17.1 us (1%)
  between operations  14.6 us (1%)
  blocking collectives  14.2 us (1%)
    all_gather x1, waiting for transfers between devices, on_device(): lax.all_gather(picture_mapping_matrix, ('dp', 'mp'), axis=0, tiled=True)  313 us
    all_gather x1, waiting for transfers between devices, on_device(): lax.all_gather(caption_mapping_matrix, ('dp', 'mp'), axis=0, tiled=True)  291 us
    unnamed x6, waiting for transfers between devices  165 us
    ppermute x48, starting transfers between devices, passed_along(): return lax.ppermute(value, axis, pairs)  105 us
    dot_general x16, matrix products, pair_terms(): image_part = jnp.dot(slope, text_emb, preferred_element_type=jnp.float32)  82.3 us
    dot_general x16, matrix products, pair_terms(): lax.dot_general(big_emb, text_emb, (((1,), (1,)), ((), ())), preferred_el...  63.8 us
    ppermute x48, waiting for transfers between devices, passed_along(): return lax.ppermute(value, axis, pairs)  62.7 us
    reduce_scatter x1, waiting for transfers between devices, on_device(): lax.psum_scatter(image_sum.astype(jnp.bfloat16), 'mp', scatter_dimension=...  42.9 us
  transfers between devices with their start and end apart: 53, of which 18 were waited for; matrix products, arithmetic and copies ran while one was open for 8% of the time, Pallas kernels for 0%

commit v1 on v0

v1 whole, which is shorter than its diff:
```python
import jax
import jax.numpy as jnp
from jax import lax
from jax.experimental import pallas as pl
from jax.experimental.pallas import tpu as pltpu
from jax.sharding import Mesh, PartitionSpec as P

AXES = ("z", "yh", "c", "yl", "x")
CHIPS = ("z", "yh", "yl", "x")
Y = ("yh", "yl")
ROWS = 128
BLOCK = 256
WIDTH = 1152
HALF = 576
STRIP = 81
TEXT_TILE = 512
BF16 = jnp.bfloat16
F32 = jnp.float32


def ring(value, axes, steps):
    count = lax.axis_size(axes)
    return lax.ppermute(value, axes, [(s, (s + steps) % count) for s in range(count)])


def swap(value, axis):
    return lax.ppermute(value, axis, [(0, 1), (1, 0)])


def spread(core):
    wanted = lax.broadcasted_iota(jnp.int32, (WIDTH, HALF), 1)
    wanted = 144 * (wanted // 72) + 72 * core + wanted % 72
    return (lax.broadcasted_iota(jnp.int32, (WIDTH, HALF), 0) == wanted).astype(BF16)


def to_bf16(a, b, dims=((1,), (0,))):
    return lax.dot_general(a, b, (dims, ((), ())), preferred_element_type=F32).astype(BF16)


def gathered(block, axis):
    previous = ring(block, axis, 1)
    following = ring(block, axis, -1)
    far_a = ring(previous[:ROWS], axis, 1)
    far_b = ring(following[ROWS:], axis, -1)
    return [block, following, far_a, far_b, previous]


def reduced(parts, axis):
    own, following, far_a, far_b, previous = parts
    late_a = ring(far_a, axis, -1)
    late_b = ring(far_b, axis, 1)
    previous = jnp.concatenate(
        [(previous[:ROWS].astype(F32) + late_a.astype(F32)).astype(BF16), previous[ROWS:]], 0
    )
    following = jnp.concatenate(
        [following[:ROWS], (following[ROWS:].astype(F32) + late_b.astype(F32)).astype(BF16)], 0
    )
    from_next = ring(previous, axis, -1)
    from_previous = ring(following, axis, 1)
    return own.astype(F32) + from_next.astype(F32) + from_previous.astype(F32)


SIZES = (256, 256, 128, 128, 256)
STARTS = (0, 256, 512, 640, 768)


def pair_kernel(*refs):
    scal, img_ids, txt_ids = refs[:3]
    img_in, txt_in = refs[3:8], refs[8:18]
    img_out, own_out, sib_out = refs[18:23], refs[23], refs[24]
    img, txt, total, sem = refs[25:]
    copies = []
    for k in range(5):
        copies.append(pltpu.make_async_copy(img_in[k], img.at[pl.ds(STARTS[k], SIZES[k])], sem.at[k]))
    for k in range(10):
        at = 1024 * (k // 5) + STARTS[k % 5]
        copies.append(pltpu.make_async_copy(txt_in[k], txt.at[pl.ds(at, SIZES[k % 5])], sem.at[5 + k]))
    for copy in copies:
        copy.start()
    for copy in copies:
        copy.wait()
    factor = scal[0]
    offset = scal[1]
    total[...] = jnp.zeros_like(total)

    def block(step):
        at = pl.multiple_of(step * TEXT_TILE, TEXT_TILE)
        text = txt[pl.ds(at, TEXT_TILE), :]
        logits = lax.dot_general(img[...], text, (((1,), (1,)), ((), ())), preferred_element_type=F32)
        logits = factor * logits + offset
        match = img_ids[...] == txt_ids[:, pl.ds(at, TEXT_TILE)]
        part = 1.0 / (1.0 + jnp.exp(jnp.where(match, logits, -logits)))
        slope = jnp.where(match, -part, part).astype(BF16)
        total[...] += jnp.dot(slope, text, preferred_element_type=F32)
        return lax.dot_general(slope, img[...], (((0,), (0,)), ((), ())), preferred_element_type=F32)

    @pl.loop(0, 2)
    def _(step):
        at = pl.multiple_of(step * TEXT_TILE, TEXT_TILE)
        own_out[pl.ds(at, TEXT_TILE), :] = block(step)

    @pl.loop(0, 2)
    def _(step):
        at = pl.multiple_of(step * TEXT_TILE, TEXT_TILE)
        sib_out[pl.ds(at, TEXT_TILE), :] = block(step + 2).astype(BF16)

    for k in range(5):
        img_out[k][...] = total[pl.ds(STARTS[k], SIZES[k]), :].astype(img_out[k].dtype)


def pairs(scal, img_ids, txt_ids, img, txt):
    vmem = pl.BlockSpec(memory_space=pltpu.VMEM)
    anywhere = pl.BlockSpec(memory_space=pl.ANY)
    out = [jax.ShapeDtypeStruct((n, WIDTH), F32 if k == 0 else BF16) for k, n in enumerate(SIZES)]
    out += [jax.ShapeDtypeStruct((1024, WIDTH), F32), jax.ShapeDtypeStruct((1024, WIDTH), BF16)]
    got = pl.pallas_call(
        pair_kernel,
        out_shape=out,
        in_specs=[pl.BlockSpec(memory_space=pltpu.SMEM), vmem, vmem] + [anywhere] * 15,
        out_specs=[vmem] * 7,
        scratch_shapes=[
            pltpu.VMEM((1024, WIDTH), BF16),
            pltpu.VMEM((2048, WIDTH), BF16),
            pltpu.VMEM((1024, WIDTH), F32),
            pltpu.SemaphoreType.DMA((15,)),
        ],
        compiler_params=pltpu.CompilerParams(vmem_limit_bytes=56 * 1024 * 1024),
        cost_estimate=pl.CostEstimate(flops=3 * 2 * 1024 * 2048 * WIDTH, bytes_accessed=20_000_000, transcendentals=4_000_000),
    )(scal, img_ids, txt_ids, *img, *txt)
    return got[:5], got[5], got[6]


def on_device(img_feat, txt_feat, img_map, txt_map, img_label, txt_label, factor, offset):
    z, yh, c, yl, x = (lax.axis_index(a) for a in AXES)
    is_img = yl == 0
    mine, other = spread(c), spread(1 - c)

    feat = jnp.concatenate([img_feat, txt_feat], 0)
    here = to_bf16(feat, mine)
    there = swap(to_bf16(feat, other), "c")
    nat = lambda v: jnp.where(is_img, v[:ROWS], v[ROWS:])
    alt = lambda v: jnp.where(is_img, v[ROWS:], v[:ROWS])
    moved = swap(jnp.concatenate([alt(here), alt(there)], 0), "yl")
    depth_rows = jnp.concatenate([nat(here), moved[:ROWS], nat(there), moved[ROWS:]], 0)

    labels = jnp.stack([img_label, txt_label])
    coded = jnp.stack([labels // 64, labels % 64], 1).astype(BF16).reshape(4, ROWS)
    both = jnp.stack([img_map.reshape(STRIP, 128), txt_map.reshape(STRIP, 128)])
    both = jnp.concatenate([both, jnp.broadcast_to(coded[None], (2, 4, 128))], 1)
    sent = jnp.broadcast_to(both[None, :, None], (8, 2, 4, STRIP + 4, 128)).reshape(64, STRIP + 4, 128)
    got = lax.all_to_all(sent, CHIPS, 0, 0, tiled=True)
    weight = got[:, :STRIP].reshape(HALF, WIDTH)
    codes = got[:, STRIP:].astype(jnp.int32).reshape(4, 2, 2, 4, 2, 2, ROWS)
    ids = codes[..., 0, :] * 64 + codes[..., 1, :]

    img_set = jnp.where(is_img, yh, 1 - yh)
    img_ids = lax.dynamic_index_in_dim(lax.dynamic_index_in_dim(ids, z, 0, False), img_set, 0, False)
    img_ids = jnp.roll(img_ids[:, :, 0], -x, axis=1).transpose(1, 0, 2).reshape(1024, 1)
    txt_ids = lax.dynamic_index_in_dim(lax.dynamic_index_in_dim(ids, yh, 1, False), x, 2, False)
    txt_ids = jnp.roll(txt_ids[:, ::-1, 1], -z, axis=0).reshape(1, 1024)
    txt_ids = jnp.concatenate([txt_ids, swap(txt_ids, "c")], 1)

    pre = jnp.dot(depth_rows, weight, preferred_element_type=F32)
    pre = pre[:BLOCK] + swap(pre[BLOCK:], "c")
    radius = jnp.sqrt(jnp.sum(pre * pre, axis=1, keepdims=True) + 1e-06)
    unit = pre / radius
    emb = unit.astype(BF16)

    shifted = ring(emb, Y, -1)
    img = gathered(jnp.where(is_img, emb, shifted), "x")
    txt = gathered(jnp.where(is_img, shifted, emb), "z")
    txt = txt + [swap(v, "c") for v in txt]

    scal = jnp.concatenate([factor, offset])
    img_parts, own, sib = pairs(scal, img_ids, txt_ids, img, txt)

    added = swap(sib, "c")
    txt_parts = []
    for k in range(5):
        span = slice(STARTS[k], STARTS[k] + SIZES[k])
        part = own[span] + added[span].astype(F32)
        txt_parts.append(part if k == 0 else part.astype(BF16))
    d_img = reduced(img_parts, "x")
    d_txt = reduced(txt_parts, "z")
    back = ring(jnp.where(is_img, d_txt, d_img).astype(BF16), Y, 1)
    grad = factor[0] * (jnp.where(is_img, d_img, d_txt) + back.astype(F32))

    d_pre = ((grad - unit * jnp.sum(unit * grad, axis=1, keepdims=True)) / radius).astype(BF16)
    d_pre = jnp.concatenate([d_pre, swap(d_pre, "c")], 0)
    d_weight = to_bf16(depth_rows, d_pre, ((0,), (0,)))
    d_weight = lax.all_to_all(d_weight.reshape(64, STRIP, 128), CHIPS, 0, 0, tiled=True)
    d_weight = jnp.sum(d_weight.reshape(8, 2, 4, STRIP, 128).astype(F32), axis=(0, 2))
    d_weight = d_weight.reshape(2, 9, WIDTH)

    d_feat = to_bf16(d_pre, weight, ((1,), (1,)))
    moved = swap(jnp.concatenate([d_feat[ROWS:BLOCK], d_feat[BLOCK + ROWS :]], 0), "yl")
    here = jnp.concatenate([d_feat[:ROWS], moved[:ROWS]], 0)
    there = swap(jnp.concatenate([d_feat[BLOCK : BLOCK + ROWS], moved[ROWS:]], 0), "c")
    d_rows = to_bf16(
        jnp.concatenate([here, there], 1), jnp.concatenate([mine, other], 1), ((1,), (1,))
    )
    nat_grad, alt_grad = d_rows[:ROWS], d_rows[ROWS:]
    img_grad = jnp.where(is_img, nat_grad, alt_grad)
    txt_grad = jnp.where(is_img, alt_grad, nat_grad)
    return (img_grad, txt_grad, d_weight[0], d_weight[1])


def solution(mesh):
    fine = Mesh(mesh.devices.reshape(4, 2, 2, 2, 4), AXES)
    rows = P(AXES, None)
    return jax.shard_map(
        on_device,
        mesh=fine,
        in_specs=(rows, rows, rows, rows, P(AXES), P(AXES), P(), P()),
        out_specs=(rows, rows, rows, rows),
        check_vma=False,
    )
```

time: 1240 us -> 228 us (0.18)
  waiting for transfers between devices: 905 us -> 95.5 us
  matrix products: 170 us -> 9.58 us
  starting transfers between devices: 106 us -> 62.1 us
  Pallas kernels: 0 us -> 26.8 us
  blocking collectives: 14.2 us -> 0 us
    all_gather x3 -> x0, waiting for transfers between devices: 635 us -> none  [the longest x1 313 us: on_device(): lax.all_gather(picture_mapping_matrix, ('dp', 'mp'), axis=0, tiled=True)]
    unnamed x6 -> x0, waiting for transfers between devices: 165 us -> none
    dot_general x54 -> x6, matrix products: 170 us -> 9.58 us  [the longest x5 7.07 us: to_bf16(): lax.dot_general(a, b, (dims, ((), ())), preferred_element_type=F32)]
    ppermute x48 -> x31, starting transfers between devices: 105 us -> 42.6 us  [the longest x18 24.3 us: ring(): lax.ppermute(value, axes, [(s, (s + steps) % count) for s in range(count)])]
    reduce_scatter x1 -> x0, waiting for transfers between devices: 42.9 us -> none  [on_device(): lax.psum_scatter(image_sum.astype(jnp.bfloat16), 'mp', scatter_dimension=...]
    pallas_call x0 -> x1, Pallas kernels: none -> 26.8 us  [pairs(): pl.pallas_call(pair_kernel, out_shape=out, in_specs=[pl.BlockSpec(memory_...]
    all_to_all x0 -> x2, starting transfers between devices: none -> 19.4 us  [the longest x1 12.1 us: on_device(): got = lax.all_to_all(sent, CHIPS, 0, 0, tiled=True)]
    ppermute x48 -> x31, waiting for transfers between devices: 62.7 us -> 79.8 us  [the longest x18 59.1 us: ring(): lax.ppermute(value, axes, [(s, (s + steps) % count) for s in range(count)])]
  transfers between devices with their start and end apart: 53 -> 33, of which waited for: 18 -> 13; matrix products, arithmetic and copies ran while one was open for 8% -> 10% of each run, Pallas kernels for 0% -> 0%
where the time goes in v1:
time: 228 us; the launch traced here: 227 us
  waiting for transfers between devices  95.5 us (42%)
  starting transfers between devices  62.1 us (27%)
  Pallas kernels  26.8 us (12%)
  local copies, waits for them, and re-layouts  19.6 us (9%)
  other arithmetic  10.6 us (5%)
  matrix products  9.58 us (4%)
  between operations  2.56 us (1%)
    ppermute x18, waiting for transfers between devices, ring(): lax.ppermute(value, axes, [(s, (s + steps) % count) for s in range(count)])  59.1 us
    pallas_call x1, Pallas kernels, pairs(): pl.pallas_call(pair_kernel, out_shape=out, in_specs=[pl.BlockSpec(memory_...  26.8 us
    ppermute x18, starting transfers between devices, ring(): lax.ppermute(value, axes, [(s, (s + steps) % count) for s in range(count)])  24.3 us
    ppermute x13, waiting for transfers between devices, swap(): return lax.ppermute(value, axis, [(0, 1), (1, 0)])  20.8 us
    ppermute x13, starting transfers between devices, swap(): return lax.ppermute(value, axis, [(0, 1), (1, 0)])  18.3 us
    all_to_all x1, waiting for transfers between devices, on_device(): lax.all_to_all(d_weight.reshape(64, STRIP, 128), CHIPS, 0, 0, tiled=True)  15.6 us
    all_to_all x1, starting transfers between devices, on_device(): got = lax.all_to_all(sent, CHIPS, 0, 0, tiled=True)  12.1 us
    all_to_all x1, starting transfers between devices, on_device(): lax.all_to_all(d_weight.reshape(64, STRIP, 128), CHIPS, 0, 0, tiled=True)  7.34 us
  transfers between devices with their start and end apart: 33, of which 13 were waited for; matrix products, arithmetic and copies ran while one was open for 10% of the time, Pallas kernels for 0%

profile of v1, /device:TPU:1, one launch (start us, length us, event | category | flops | bytes accessed | tf_op | source)
XLA Modules:
  0.0 226.7 jit_solution(12696624859223240410)
XLA Ops:
  1.3 0.8 stack_reshape.6
  2.2 0.8 stack_reshape.7
  3.0 1.3 broadcast_in_dim.5
  4.4 12.1 %all-to-all-start = ((bf16[64,85,128]{2,1,0:T(8,128)(2,1)}), bf16[64,85,128]{2,1,0:T(8,128)(2,1)S(1)}, u32[]{:S(2)}, u32[]{:S(2)}) async-start(bf16[64,85,128]{2,1,0:T(8,128)(2,1)} %bitcast.28), calls=%async_computation | async-start | bytes 2883584 | tf_op jit(solution)/shard_map/all_to_all | solution.py:151
  16.6 1.0 fusion.4
  17.6 1.7 convolution_convert_fusion.2
  19.3 1.0 collective-permute-start.1
  20.2 1.7 convolution_convert_fusion.3
  21.9 1.0 broadcast_select_fusion.7
  23.0 1.4 collective-permute-start.2
  24.4 15.5 %collective-permute-done.2 = bf16[256,576]{0,1:T(8,128)(2,1)S(1)} collective-permute-done((bf16[256,576]{0,1:T(8,128)(2,1)S(1)}, bf16[256,576]{0,1:T(8,128)(2,1)S(1)}, u32[]{:S(2)}, u32[]{:S(2)}) %collective-permute-start.2) | collective-permute-done | bytes 294944 | tf_op jit(solution)/shard_map/ppermute | solution.py:27
  39.9 2.5 %reshape.283 = bf16[576,1152]{1,0:T(8,128)(2,1)} reshape(bf16[64,81,128]{2,1,0:T(8,128)(2,1)S(1)} %bitcast.27) | data formatting | bytes 2654208 | tf_op jit(solution)/shard_map/reshape | solution.py:152
  42.4 2.5 %fusion.14 = f32[512,1152]{1,0:T(8,128)S(1)} fusion(bf16[576,1152]{1,0:T(8,128)(2,1)} %reshape.283, bf16[128,576]{0,1:T(8,128)(2,1)S(1)} %get-tuple-element.41, bf16[128,576]{0,1:T(8,128)(2,1)S(1)} %get-tuple-element.42, bf16[128,576]{0,1:T(8,128)(2,1)S(1)} %get-tuple-element.40, bf16[128,576]{0,1:T(8,128)(2,1)S(1)} %get-tuple-element.38), kind=kOutput, calls=%fused_computation.54 | convolution fusion | flops 681836544 | bytes 4276224 | tf_op jit(solution)/shard_map/dot_general | solution.py:163
  45.0 1.0 collective-permute-start.3
  46.0 2.5 %collective-permute-done.3 = f32[256,1152]{1,0:T(8,128)S(1)} collective-permute-done((f32[256,1152]{1,0:T(8,128)S(1)}, f32[256,1152]{1,0:T(8,128)S(1)}, u32[]{:S(2)}, u32[]{:S(2)}) %collective-permute-start.3) | collective-permute-done | bytes 1179680 | tf_op jit(solution)/shard_map/ppermute | solution.py:27
  48.9 1.9 collective-permute-start.4
  50.8 12.8 %collective-permute-done.4 = bf16[256,1152]{1,0:T(8,128)(2,1)S(1)} collective-permute-done((bf16[256,1152]{1,0:T(8,128)(2,1)S(1)}, bf16[256,1152]{1,0:T(8,128)(2,1)S(1)}, u32[]{:S(2)}, u32[]{:S(2)}) %collective-permute-start.4) | collective-permute-done | bytes 589856 | tf_op jit(solution)/shard_map/ppermute | solution.py:23
  63.5 1.1 broadcast_select_fusion
  64.7 1.2 collective-permute-start.6
  65.8 1.2 collective-permute-start.10
  67.0 1.5 collective-permute-start.9
  68.5 1.5 collective-permute-start.5
  70.0 2.3 %collective-permute-start.13 = (bf16[256,1152]{1,0:T(8,128)(2,1)}, bf16[256,1152]{1,0:T(8,128)(2,1)}, u32[]{:S(2)}, u32[]{:S(2)}) collective-permute-start(bf16[256,1152]{1,0:T(8,128)(2,1)} %get-tuple-element.28.refs_8_), channel_id=1, source_target_pairs={{0,8},{8,0},{1,9},{9,1},{2,10},{10,2},{3,11},{11,3},{4,12},{12,4},... | collective-permute-start | bytes 1769480 | tf_op jit(solution)/shard_map/ppermute | solution.py:27
  72.6 7.3 %collective-permute-done.6.refs_7_ = bf16[256,1152]{1,0:T(8,128)(2,1)} collective-permute-done((bf16[256,1152]{1,0:T(8,128)(2,1)}, bf16[256,1152]{1,0:T(8,128)(2,1)}, u32[]{:S(2)}, u32[]{:S(2)}) %collective-permute-start.6) | collective-permute-done | bytes 589856 | tf_op jit(solution)/shard_map/ppermute | solution.py:23
  79.8 2.1 collective-permute-start
  81.9 1.0 slice.204
  83.0 1.0 slice.206
  84.0 1.3 collective-permute-start.11
  85.3 1.0 slice.207
  86.3 1.5 collective-permute-start.12
  87.8 2.1 collective-permute-start.17
  92.0 1.0 slice.205
  93.0 1.6 collective-permute-start.8
  95.9 1.1 copy.24.refs_1_
  97.6 3.3 %collective-permute-done.8.refs_6_ = bf16[128,1152]{1,0:T(8,128)(2,1)S(1)} collective-permute-done((bf16[128,1152]{1,0:T(8,128)(2,1)S(1)}, bf16[128,1152]{1,0:T(8,128)(2,1)S(1)}, u32[]{:S(2)}, u32[]{:S(2)}) %collective-permute-start.8) | collective-permute-done | bytes 294944 | tf_op jit(solution)/shard_map/ppermute | solution.py:23
  102.4 26.8 %shard_map.111 = (f32[256,1152]{1,0:T(8,128)}, bf16[256,1152]{1,0:T(8,128)(2,1)}, bf16[128,1152]{1,0:T(8,128)(2,1)}, bf16[128,1152]{1,0:T(8,128)(2,1)}, bf16[256...) custom-call(f32[2]{0:T(128)} %pad_maximum_fusion.15.refs_0_, s32[1024,1]{1,0:T(8,128)} %copy.24.refs_1_, ...), custom_call_target="tpu_custom_call" | custom-call | flops 14495514624 | bytes 20000000 | tf_op jit(solution)/shard_map/pallas_call | solution.py:116
  129.2 1.7 collective-permute-start.22
  130.9 0.9 collective-permute-start.20
  131.8 1.1 slice.163
  132.8 1.1 slice.164
  134.0 1.9 collective-permute-start.18
  135.9 5.1 %collective-permute-done.20 = bf16[128,1152]{1,0:T(8,128)(2,1)S(1)} collective-permute-done((bf16[128,1152]{1,0:T(8,128)(2,1)}, bf16[128,1152]{1,0:T(8,128)(2,1)S(1)}, u32[]{:S(2)}, u32[]{:S(2)}) %collective-permute-start.20) | collective-permute-done | bytes 294944 | tf_op jit(solution)/shard_map/ppermute | solution.py:23
  141.0 1.0 add_convert_fusion.6
  142.6 3.4 %collective-permute-start.19 = (bf16[256,1152]{1,0:T(8,128)(2,1)S(1)}, bf16[256,1152]{1,0:T(8,128)(2,1)S(1)}, u32[]{:S(2)}, u32[]{:S(2)}) collective-permute-start(bf16[256,1152]{1,0:T(8,128)(2,1)S(1)} %pad_maximum_fusion.4), channel_id=1, source_target_pairs={{0,3},{1,0},{2,1},{3,2},{4,7},{5,4},{6,5},{7,6},{8,11},{9,8},{10,9... | collective-permute-start | bytes 1769480 | tf_op jit(solution)/shard_map/ppermute | solution.py:23
  146.1 2.5 %collective-permute-start.23 = (bf16[128,1152]{1,0:T(8,128)(2,1)S(1)}, bf16[128,1152]{1,0:T(8,128)(2,1)S(1)}, u32[]{:S(2)}, u32[]{:S(2)}) collective-permute-start(bf16[128,1152]{1,0:T(8,128)(2,1)S(1)} %get-tuple-element.24), channel_id=1, source_target_pairs={{0,96},{32,0},{64,32},{96,64},{1,97},{33,1},{65,33},{97,65},{2,98}... | collective-permute-start | bytes 884744 | tf_op jit(solution)/shard_map/ppermute | solution.py:23
  148.9 7.7 %collective-permute-done.25 = bf16[128,1152]{1,0:T(8,128)(2,1)S(1)} collective-permute-done((bf16[128,1152]{1,0:T(8,128)(2,1)S(1)}, bf16[128,1152]{1,0:T(8,128)(2,1)S(1)}, u32[]{:S(2)}, u32[]{:S(2)}) %collective-permute-start.25) | collective-permute-done | bytes 294944 | tf_op jit(solution)/shard_map/ppermute | solution.py:23
  157.0 2.7 %collective-permute-start.24 = (bf16[256,1152]{1,0:T(8,128)(2,1)S(1)}, bf16[256,1152]{1,0:T(8,128)(2,1)S(1)}, u32[]{:S(2)}, u32[]{:S(2)}) collective-permute-start(bf16[256,1152]{1,0:T(8,128)(2,1)S(1)} %pad_maximum_fusion.6), channel_id=1, source_target_pairs={{0,96},{32,0},{64,32},{96,64},{1,97},{33,1},{65,33},{97,65},{2,98}... | collective-permute-start | bytes 1769480 | tf_op jit(solution)/shard_map/ppermute | solution.py:23
  159.7 10.5 %collective-permute-done.26 = bf16[256,1152]{1,0:T(8,128)(2,1)S(1)} collective-permute-done((bf16[256,1152]{1,0:T(8,128)(2,1)S(1)}, bf16[256,1152]{1,0:T(8,128)(2,1)S(1)}, u32[]{:S(2)}, u32[]{:S(2)}) %collective-permute-start.26) | collective-permute-done | bytes 589856 | tf_op jit(solution)/shard_map/ppermute | solution.py:23
  170.7 1.0 collective-permute-start.27
  171.7 12.1 %collective-permute-done.27 = bf16[256,1152]{1,0:T(8,128)(2,1)S(1)} collective-permute-done((bf16[256,1152]{1,0:T(8,128)(2,1)S(1)}, bf16[256,1152]{1,0:T(8,128)(2,1)S(1)}, u32[]{:S(2)}, u32[]{:S(2)}) %collective-permute-start.27) | collective-permute-done | bytes 589856 | tf_op jit(solution)/shard_map/ppermute | solution.py:23
  183.8 0.7 multiply_reduce_fusion
  184.8 4.3 %collective-permute-start.28 = (bf16[256,1152]{1,0:T(8,128)(2,1)S(1)}, bf16[256,1152]{1,0:T(8,128)(2,1)S(1)}, u32[]{:S(2)}, u32[]{:S(2)}) collective-permute-start(bf16[256,1152]{1,0:T(8,128)(2,1)S(1)} %divide_convert_fusion), channel_id=1, source_target_pairs={{0,8},{8,0},{1,9},{9,1},{2,10},{10,2},{3,11},{11,3},{4,12},{12,4},... | collective-permute-start | bytes 1769480 | tf_op jit(solution)/shard_map/ppermute | solution.py:27
  189.1 1.6 collective-permute-done.28
  190.7 1.0 convolution_convert_fusion.1
  191.8 0.7 pad_maximum_fusion.9
  192.8 0.9 convolution_convert_fusion
  193.7 2.4 %reshape.284 = bf16[64,81,128]{2,1,0:T(8,128)(2,1)} reshape(bf16[576,1152]{1,0:T(8,128)(2,1)S(1)} %convolution_convert_fusion) | data formatting | bytes 2654208 | tf_op jit(solution)/shard_map/reshape | solution.py:191
  196.1 7.3 %all-to-all-start.1 = ((bf16[64,81,128]{2,1,0:T(8,128)(2,1)}), bf16[64,81,128]{2,1,0:T(8,128)(2,1)S(1)}, u32[]{:S(2)}, u32[]{:S(2)}) async-start(bf16[64,81,128]{2,1,0:T(8,128)(2,1)} %reshape.284), calls=%async_computation.1 | async-start | bytes 2883584 | tf_op jit(solution)/shard_map/all_to_all | solution.py:191
  203.5 1.1 fusion.33
  204.6 1.0 collective-permute-start.30
  205.6 1.2 collective-permute-done.30
  206.8 1.8 fusion.6
  208.7 0.9 broadcast_select_fusion.2
  209.5 15.6 %all-to-all-done.1 = bf16[64,81,128]{2,1,0:T(8,128)(2,1)S(1)} async-done(((bf16[64,81,128]{2,1,0:T(8,128)(2,1)}), bf16[64,81,128]{2,1,0:T(8,128)(2,1)S(1)}, u32[]{:S(2)}, u32[]{:S(2)}) %all-to-all-start.1) | async-done | bytes 1327136 | tf_op jit(solution)/shard_map/all_to_all | solution.py:191
  (114 shorter events, 9.7 us)
Async XLA Ops:
  4.4 12.2 %copy-start.6 = (bf16[128,1152]{1,0:T(8,128)(2,1)S(1)}, bf16[128,1152]{1,0:T(8,128)(2,1)}, u32[]{:S(2)}) copy-start(bf16[128,1152]{1,0:T(8,128)(2,1)} %param.8) | copy-start | bytes 884740
  4.4 12.2 %copy-start.7 = (bf16[128,1152]{1,0:T(8,128)(2,1)S(1)}, bf16[128,1152]{1,0:T(8,128)(2,1)}, u32[]{:S(2)}) copy-start(bf16[128,1152]{1,0:T(8,128)(2,1)} %param.9) | copy-start | bytes 884740
  4.4 35.5 %all-to-all-start = ((bf16[64,85,128]{2,1,0:T(8,128)(2,1)}), bf16[64,85,128]{2,1,0:T(8,128)(2,1)S(1)}, u32[]{:S(2)}, u32[]{:S(2)}) async-start(bf16[64,85,128]{2,1,0:T(8,128)(2,1)} %bitcast.28), calls=%async_computation | async-start | bytes 2883584 | tf_op jit(solution)/shard_map/all_to_all | solution.py:151
  17.6 4.3 %copy-start.3 = (pred[1152,576]{1,0:T(32,128)(4,1)}, pred[1152,576]{1,0:T(32,128)(4,1)S(1)}, u32[]{:S(2)}) copy-start(pred[1152,576]{1,0:T(32,128)(4,1)S(1)} %get-tuple-element.47) | copy-start | bytes 1990660
  19.3 3.6 %collective-permute-start.1 = (bf16[256,576]{0,1:T(8,128)(2,1)}, bf16[256,576]{0,1:T(8,128)(2,1)S(1)}, u32[]{:S(2)}, u32[]{:S(2)}) collective-permute-start(bf16[256,576]{0,1:T(8,128)(2,1)} %convolution_convert_fusion.2), channel_id=1, source_target_pairs={{0,8},{8,0},{1,9},{9,1},{2,10},{10,2},{3,11},{11,3},{4,12},{12,4},... | collective-permute-start | bytes 884744 | tf_op jit(solution)/shard_map/ppermute | solution.py:27
  22.9 19.4 %copy-start.8 = (bf16[128,576]{0,1:T(8,128)(2,1)}, bf16[128,576]{0,1:T(8,128)(2,1)S(1)}, u32[]{:S(2)}) copy-start(bf16[128,576]{0,1:T(8,128)(2,1)S(1)} %get-tuple-element.42) | copy-start | bytes 442372
  23.0 16.8 %collective-permute-start.2 = (bf16[256,576]{0,1:T(8,128)(2,1)S(1)}, bf16[256,576]{0,1:T(8,128)(2,1)S(1)}, u32[]{:S(2)}, u32[]{:S(2)}) collective-permute-start(bf16[256,576]{0,1:T(8,128)(2,1)S(1)} %pad_maximum_fusion.8), channel_id=1, source_target_pairs={{0,4},{4,0},{1,5},{5,1},{2,6},{6,2},{3,7},{7,3},{8,12},{12,8},{9,1... | collective-permute-start | bytes 884744 | tf_op jit(solution)/shard_map/ppermute | solution.py:27
  39.8 2.5 %copy-start.10 = (bf16[128,576]{0,1:T(8,128)(2,1)}, bf16[128,576]{0,1:T(8,128)(2,1)S(1)}, u32[]{:S(2)}) copy-start(bf16[128,576]{0,1:T(8,128)(2,1)S(1)} %get-tuple-element.40) | copy-start | bytes 442372
  39.9 2.5 %copy-start.12 = (bf16[128,576]{0,1:T(8,128)(2,1)}, bf16[128,576]{0,1:T(8,128)(2,1)S(1)}, u32[]{:S(2)}) copy-start(bf16[128,576]{0,1:T(8,128)(2,1)S(1)} %get-tuple-element.41) | copy-start | bytes 442372
  45.0 3.5 %collective-permute-start.3 = (f32[256,1152]{1,0:T(8,128)S(1)}, f32[256,1152]{1,0:T(8,128)S(1)}, u32[]{:S(2)}, u32[]{:S(2)}) collective-permute-start(f32[256,1152]{1,0:T(8,128)S(1)} %slice.203), channel_id=1, source_target_pairs={{0,8},{8,0},{1,9},{9,1},{2,10},{10,2},{3,11},{11,3},{4,12},{12,4},... | collective-permute-start | bytes 3538952 | tf_op jit(solution)/shard_map/ppermute | solution.py:27
  48.9 14.6 %collective-permute-start.4 = (bf16[256,1152]{1,0:T(8,128)(2,1)S(1)}, bf16[256,1152]{1,0:T(8,128)(2,1)S(1)}, u32[]{:S(2)}, u32[]{:S(2)}) collective-permute-start(bf16[256,1152]{1,0:T(8,128)(2,1)S(1)} %get-tuple-element.20), channel_id=1, source_target_pairs={{0,20},{4,0},{16,4},{20,16},{1,21},{5,1},{17,5},{21,17},{2,22},{6,... | collective-permute-start | bytes 1769480 | tf_op jit(solution)/shard_map/ppermute | solution.py:23
  64.7 15.1 %collective-permute-start.6 = (bf16[256,1152]{1,0:T(8,128)(2,1)}, bf16[256,1152]{1,0:T(8,128)(2,1)}, u32[]{:S(2)}, u32[]{:S(2)}) collective-permute-start(bf16[256,1152]{1,0:T(8,128)(2,1)} %get-tuple-element.29.refs_3_), channel_id=1, source_target_pairs={{0,1},{1,2},{2,3},{3,0},{4,5},{5,6},{6,7},{7,4},{8,9},{9,10},{10,1... | collective-permute-start | bytes 1769480 | tf_op jit(solution)/shard_map/ppermute | solution.py:23
  65.8 17.1 %collective-permute-start.10 = (bf16[256,1152]{1,0:T(8,128)(2,1)}, bf16[256,1152]{1,0:T(8,128)(2,1)}, u32[]{:S(2)}, u32[]{:S(2)}) collective-permute-start(bf16[256,1152]{1,0:T(8,128)(2,1)} %get-tuple-element.28.refs_8_), channel_id=1, source_target_pairs={{0,32},{32,64},{64,96},{96,0},{1,33},{33,65},{65,97},{97,1},{2,34}... | collective-permute-start | bytes 1769480 | tf_op jit(solution)/shard_map/ppermute | solution.py:23
  67.0 17.0 %collective-permute-start.9 = (bf16[256,1152]{1,0:T(8,128)(2,1)}, bf16[256,1152]{1,0:T(8,128)(2,1)}, u32[]{:S(2)}, u32[]{:S(2)}) collective-permute-start(bf16[256,1152]{1,0:T(8,128)(2,1)} %get-tuple-element.28.refs_8_), channel_id=1, source_target_pairs={{0,96},{32,0},{64,32},{96,64},{1,97},{33,1},{65,33},{97,65},{2,98}... | collective-permute-start | bytes 1769480 | tf_op jit(solution)/shard_map/ppermute | solution.py:23
  68.5 19.3 %collective-permute-start.5 = (bf16[256,1152]{1,0:T(8,128)(2,1)}, bf16[256,1152]{1,0:T(8,128)(2,1)}, u32[]{:S(2)}, u32[]{:S(2)}) collective-permute-start(bf16[256,1152]{1,0:T(8,128)(2,1)} %get-tuple-element.29.refs_3_), channel_id=1, source_target_pairs={{0,3},{1,0},{2,1},{3,2},{4,7},{5,4},{6,5},{7,6},{8,11},{9,8},{10,9... | collective-permute-start | bytes 1769480 | tf_op jit(solution)/shard_map/ppermute | solution.py:23
  70.0 19.9 %collective-permute-start.13 = (bf16[256,1152]{1,0:T(8,128)(2,1)}, bf16[256,1152]{1,0:T(8,128)(2,1)}, u32[]{:S(2)}, u32[]{:S(2)}) collective-permute-start(bf16[256,1152]{1,0:T(8,128)(2,1)} %get-tuple-element.28.refs_8_), channel_id=1, source_target_pairs={{0,8},{8,0},{1,9},{9,1},{2,10},{10,2},{3,11},{11,3},{4,12},{12,4},... | collective-permute-start | bytes 1769480 | tf_op jit(solution)/shard_map/ppermute | solution.py:27
  79.8 6.5 %collective-permute-start = (s32[1,1024]{1,0:T(1,128)S(1)}, s32[1,1024]{1,0:T(1,128)S(1)}, u32[]{:S(2)}, u32[]{:S(2)}) collective-permute-start(s32[1,1024]{1,0:T(1,128)S(1)} %bitcast.36), channel_id=1, source_target_pairs={{0,8},{8,0},{1,9},{9,1},{2,10},{10,2},{3,11},{11,3},{4,12},{12,4},... | collective-permute-start | bytes 12296 | tf_op jit(solution)/shard_map/ppermute | solution.py:27
  82.9 10.0 %collective-permute-start.7 = (bf16[128,1152]{1,0:T(8,128)(2,1)S(1)}, bf16[128,1152]{1,0:T(8,128)(2,1)}, u32[]{:S(2)}, u32[]{:S(2)}) collective-permute-start(bf16[128,1152]{1,0:T(8,128)(2,1)S(1)} %slice.204), channel_id=1, source_target_pairs={{0,1},{1,2},{2,3},{3,0},{4,5},{5,6},{6,7},{7,4},{8,9},{9,10},{10,1... | collective-permute-start | bytes 884744 | tf_op jit(solution)/shard_map/ppermute | solution.py:23
  84.0 10.5 %collective-permute-start.11 = (bf16[128,1152]{1,0:T(8,128)(2,1)S(1)}, bf16[128,1152]{1,0:T(8,128)(2,1)}, u32[]{:S(2)}, u32[]{:S(2)}) collective-permute-start(bf16[128,1152]{1,0:T(8,128)(2,1)S(1)} %slice.206), channel_id=1, source_target_pairs={{0,32},{32,64},{64,96},{96,0},{1,33},{33,65},{65,97},{97,1},{2,34}... | collective-permute-start | bytes 884744 | tf_op jit(solution)/shard_map/ppermute | solution.py:23
  86.3 9.0 %collective-permute-start.12 = (bf16[128,1152]{1,0:T(8,128)(2,1)S(1)}, bf16[128,1152]{1,0:T(8,128)(2,1)}, u32[]{:S(2)}, u32[]{:S(2)}) collective-permute-start(bf16[128,1152]{1,0:T(8,128)(2,1)S(1)} %slice.207), channel_id=1, source_target_pairs={{0,96},{32,0},{64,32},{96,64},{1,97},{33,1},{65,33},{97,65},{2,98}... | collective-permute-start | bytes 884744 | tf_op jit(solution)/shard_map/ppermute | solution.py:23
  87.8 13.0 %collective-permute-start.17 = (bf16[256,1152]{1,0:T(8,128)(2,1)}, bf16[256,1152]{1,0:T(8,128)(2,1)}, u32[]{:S(2)}, u32[]{:S(2)}) collective-permute-start(bf16[256,1152]{1,0:T(8,128)(2,1)} %collective-permute-done.10.refs_12_), channel_id=1, source_target_pairs={{0,8},{8,0},{1,9},{9,1},{2,10},{10,2},{3,11},{11,3},{4,12},{12,4},... | collective-permute-start | bytes 1769480 | tf_op jit(solution)/shard_map/ppermute | solution.py:27
  90.0 10.9 %collective-permute-start.14 = (bf16[256,1152]{1,0:T(8,128)(2,1)}, bf16[256,1152]{1,0:T(8,128)(2,1)}, u32[]{:S(2)}, u32[]{:S(2)}) collective-permute-start(bf16[256,1152]{1,0:T(8,128)(2,1)} %collective-permute-done.9.refs_9_), channel_id=1, source_target_pairs={{0,8},{8,0},{1,9},{9,1},{2,10},{10,2},{3,11},{11,3},{4,12},{12,4},... | collective-permute-start | bytes 1769480 | tf_op jit(solution)/shard_map/ppermute | solution.py:27
  93.0 7.9 %collective-permute-start.8 = (bf16[128,1152]{1,0:T(8,128)(2,1)S(1)}, bf16[128,1152]{1,0:T(8,128)(2,1)S(1)}, u32[]{:S(2)}, u32[]{:S(2)}) collective-permute-start(bf16[128,1152]{1,0:T(8,128)(2,1)S(1)} %slice.205), channel_id=1, source_target_pairs={{0,3},{1,0},{2,1},{3,2},{4,7},{5,4},{6,5},{7,6},{8,11},{9,8},{10,9... | collective-permute-start | bytes 884744 | tf_op jit(solution)/shard_map/ppermute | solution.py:23
  94.6 6.3 %collective-permute-start.15 = (bf16[128,1152]{1,0:T(8,128)(2,1)}, bf16[128,1152]{1,0:T(8,128)(2,1)S(1)}, u32[]{:S(2)}, u32[]{:S(2)}) collective-permute-start(bf16[128,1152]{1,0:T(8,128)(2,1)} %collective-permute-done.11.refs_10_), channel_id=1, source_target_pairs={{0,8},{8,0},{1,9},{9,1},{2,10},{10,2},{3,11},{11,3},{4,12},{12,4},... | collective-permute-start | bytes 884744 | tf_op jit(solution)/shard_map/ppermute | solution.py:27
  95.3 5.6 %collective-permute-start.16 = (bf16[128,1152]{1,0:T(8,128)(2,1)}, bf16[128,1152]{1,0:T(8,128)(2,1)S(1)}, u32[]{:S(2)}, u32[]{:S(2)}) collective-permute-start(bf16[128,1152]{1,0:T(8,128)(2,1)} %collective-permute-done.12.refs_11_), channel_id=1, source_target_pairs={{0,8},{8,0},{1,9},{9,1},{2,10},{10,2},{3,11},{11,3},{4,12},{12,4},... | collective-permute-start | bytes 884744 | tf_op jit(solution)/shard_map/ppermute | solution.py:27
  100.8 0.7 copy-start.14
  100.9 0.8 copy-start.15
  101.7 0.7 copy-start.16
  129.2 16.8 %collective-permute-start.22 = (bf16[1024,1152]{1,0:T(8,128)(2,1)}, bf16[1024,1152]{1,0:T(8,128)(2,1)S(1)}, u32[]{:S(2)}, u32[]{:S(2)}) collective-permute-start(bf16[1024,1152]{1,0:T(8,128)(2,1)} %get-tuple-element.17), channel_id=1, source_target_pairs={{0,8},{8,0},{1,9},{9,1},{2,10},{10,2},{3,11},{11,3},{4,12},{12,4},... | collective-permute-start | bytes 7077896 | tf_op jit(solution)/shard_map/ppermute | solution.py:27
  130.9 10.1 %collective-permute-start.20 = (bf16[128,1152]{1,0:T(8,128)(2,1)}, bf16[128,1152]{1,0:T(8,128)(2,1)S(1)}, u32[]{:S(2)}, u32[]{:S(2)}) collective-permute-start(bf16[128,1152]{1,0:T(8,128)(2,1)} %get-tuple-element.15), channel_id=1, source_target_pairs={{0,1},{1,2},{2,3},{3,0},{4,5},{5,6},{6,7},{7,4},{8,9},{9,10},{10,1... | collective-permute-start | bytes 884744 | tf_op jit(solution)/shard_map/ppermute | solution.py:23
  131.8 10.7 %copy-start.5 = (bf16[256,1152]{1,0:T(8,128)(2,1)S(1)}, bf16[256,1152]{1,0:T(8,128)(2,1)}, u32[]{:S(2)}) copy-start(bf16[256,1152]{1,0:T(8,128)(2,1)} %get-tuple-element.12) | copy-start | bytes 1769476
  132.8 13.2 %copy-start = (f32[1024,1152]{1,0:T(8,128)S(1)}, f32[1024,1152]{1,0:T(8,128)}, u32[]{:S(2)}) copy-start(f32[1024,1152]{1,0:T(8,128)} %get-tuple-element.16) | copy-start | bytes 14155780
  134.0 8.5 %collective-permute-start.18 = (bf16[128,1152]{1,0:T(8,128)(2,1)}, bf16[128,1152]{1,0:T(8,128)(2,1)S(1)}, u32[]{:S(2)}, u32[]{:S(2)}) collective-permute-start(bf16[128,1152]{1,0:T(8,128)(2,1)} %get-tuple-element.13), channel_id=1, source_target_pairs={{0,3},{1,0},{2,1},{3,2},{4,7},{5,4},{6,5},{7,6},{8,11},{9,8},{10,9... | collective-permute-start | bytes 884744 | tf_op jit(solution)/shard_map/ppermute | solution.py:23
  142.1 17.7 %collective-permute-start.21 = (bf16[256,1152]{1,0:T(8,128)(2,1)S(1)}, bf16[256,1152]{1,0:T(8,128)(2,1)S(1)}, u32[]{:S(2)}, u32[]{:S(2)}) collective-permute-start(bf16[256,1152]{1,0:T(8,128)(2,1)S(1)} %pad_maximum_fusion.5), channel_id=1, source_target_pairs={{0,1},{1,2},{2,3},{3,0},{4,5},{5,6},{6,7},{7,4},{8,9},{9,10},{10,1... | collective-permute-start | bytes 1769480 | tf_op jit(solution)/shard_map/ppermute | solution.py:23
  142.6 17.1 %collective-permute-start.19 = (bf16[256,1152]{1,0:T(8,128)(2,1)S(1)}, bf16[256,1152]{1,0:T(8,128)(2,1)S(1)}, u32[]{:S(2)}, u32[]{:S(2)}) collective-permute-start(bf16[256,1152]{1,0:T(8,128)(2,1)S(1)} %pad_maximum_fusion.4), channel_id=1, source_target_pairs={{0,3},{1,0},{2,1},{3,2},{4,7},{5,4},{6,5},{7,6},{8,11},{9,8},{10,9... | collective-permute-start | bytes 1769480 | tf_op jit(solution)/shard_map/ppermute | solution.py:23
  146.1 10.7 %collective-permute-start.23 = (bf16[128,1152]{1,0:T(8,128)(2,1)S(1)}, bf16[128,1152]{1,0:T(8,128)(2,1)S(1)}, u32[]{:S(2)}, u32[]{:S(2)}) collective-permute-start(bf16[128,1152]{1,0:T(8,128)(2,1)S(1)} %get-tuple-element.24), channel_id=1, source_target_pairs={{0,96},{32,0},{64,32},{96,64},{1,97},{33,1},{65,33},{97,65},{2,98}... | collective-permute-start | bytes 884744 | tf_op jit(solution)/shard_map/ppermute | solution.py:23
  148.7 8.0 %collective-permute-start.25 = (bf16[128,1152]{1,0:T(8,128)(2,1)S(1)}, bf16[128,1152]{1,0:T(8,128)(2,1)S(1)}, u32[]{:S(2)}, u32[]{:S(2)}) collective-permute-start(bf16[128,1152]{1,0:T(8,128)(2,1)S(1)} %get-tuple-element.25), channel_id=1, source_target_pairs={{0,32},{32,64},{64,96},{96,0},{1,33},{33,65},{65,97},{97,1},{2,34}... | collective-permute-start | bytes 884744 | tf_op jit(solution)/shard_map/ppermute | solution.py:23
  156.8 13.5 %copy-start.1 = (f32[256,1152]{1,0:T(8,128)S(1)}, f32[256,1152]{1,0:T(8,128)}, u32[]{:S(2)}) copy-start(f32[256,1152]{1,0:T(8,128)} %get-tuple-element.11) | copy-start | bytes 3538948
  156.8 13.4 %collective-permute-start.26 = (bf16[256,1152]{1,0:T(8,128)(2,1)S(1)}, bf16[256,1152]{1,0:T(8,128)(2,1)S(1)}, u32[]{:S(2)}, u32[]{:S(2)}) collective-permute-start(bf16[256,1152]{1,0:T(8,128)(2,1)S(1)} %pad_maximum_fusion.7), channel_id=1, source_target_pairs={{0,32},{32,64},{64,96},{96,0},{1,33},{33,65},{65,97},{97,1},{2,34}... | collective-permute-start | bytes 1769480 | tf_op jit(solution)/shard_map/ppermute | solution.py:23
  157.0 13.2 %collective-permute-start.24 = (bf16[256,1152]{1,0:T(8,128)(2,1)S(1)}, bf16[256,1152]{1,0:T(8,128)(2,1)S(1)}, u32[]{:S(2)}, u32[]{:S(2)}) collective-permute-start(bf16[256,1152]{1,0:T(8,128)(2,1)S(1)} %pad_maximum_fusion.6), channel_id=1, source_target_pairs={{0,96},{32,0},{64,32},{96,64},{1,97},{33,1},{65,33},{97,65},{2,98}... | collective-permute-start | bytes 1769480 | tf_op jit(solution)/shard_map/ppermute | solution.py:23
  170.7 13.1 %collective-permute-start.27 = (bf16[256,1152]{1,0:T(8,128)(2,1)S(1)}, bf16[256,1152]{1,0:T(8,128)(2,1)S(1)}, u32[]{:S(2)}, u32[]{:S(2)}) collective-permute-start(bf16[256,1152]{1,0:T(8,128)(2,1)S(1)} %select_convert_fusion), channel_id=1, source_target_pairs={{0,4},{4,16},{16,20},{20,0},{1,5},{5,17},{17,21},{21,1},{2,6},{6,1... | collective-permute-start | bytes 1769480 | tf_op jit(solution)/shard_map/ppermute | solution.py:23
  184.6 6.2 %copy-start.2 = (bf16[576,1152]{1,0:T(8,128)(2,1)S(1)}, bf16[576,1152]{1,0:T(8,128)(2,1)}, u32[]{:S(2)}) copy-start(bf16[576,1152]{1,0:T(8,128)(2,1)} %reshape.283) | copy-start | bytes 3981316
  184.8 5.9 %collective-permute-start.28 = (bf16[256,1152]{1,0:T(8,128)(2,1)S(1)}, bf16[256,1152]{1,0:T(8,128)(2,1)S(1)}, u32[]{:S(2)}, u32[]{:S(2)}) collective-permute-start(bf16[256,1152]{1,0:T(8,128)(2,1)S(1)} %divide_convert_fusion), channel_id=1, source_target_pairs={{0,8},{8,0},{1,9},{9,1},{2,10},{10,2},{3,11},{11,3},{4,12},{12,4},... | collective-permute-start | bytes 1769480 | tf_op jit(solution)/shard_map/ppermute | solution.py:27
  191.7 0.9 copy-start.9
  191.7 1.0 copy-start.11
  191.7 1.1 copy-start.13
  192.6 10.9 %collective-permute-start.29 = (bf16[256,576]{0,1:T(8,128)(2,1)}, bf16[256,576]{0,1:T(8,128)(2,1)}, u32[]{:S(2)}, u32[]{:S(2)}) collective-permute-start(bf16[256,576]{0,1:T(8,128)(2,1)} %pad_maximum_fusion.9), channel_id=1, source_target_pairs={{0,4},{4,0},{1,5},{5,1},{2,6},{6,2},{3,7},{7,3},{8,12},{12,8},{9,1... | collective-permute-start | bytes 884744 | tf_op jit(solution)/shard_map/ppermute | solution.py:27
  196.1 29.1 %all-to-all-start.1 = ((bf16[64,81,128]{2,1,0:T(8,128)(2,1)}), bf16[64,81,128]{2,1,0:T(8,128)(2,1)S(1)}, u32[]{:S(2)}, u32[]{:S(2)}) async-start(bf16[64,81,128]{2,1,0:T(8,128)(2,1)} %reshape.284), calls=%async_computation.1 | async-start | bytes 2883584 | tf_op jit(solution)/shard_map/all_to_all | solution.py:191
  203.5 3.4 %copy-start.4 = (pred[1152,576]{1,0:T(32,128)(4,1)S(1)}, pred[1152,576]{1,0:T(32,128)(4,1)}, u32[]{:S(2)}) copy-start(pred[1152,576]{1,0:T(32,128)(4,1)} %copy-done.3) | copy-start | bytes 1990660
  204.6 2.2 collective-permute-start.30
